TPU v7x, 32 devices: a whole 2x2x4 slice. The times are simulated.
32 devices in a mesh: grp: 2 (over y), row: 8 (over z, x), col: 1, sub: 2 (over core).
Axes of the slice: x: 2, y: 2, z: 4, core: 2. Of those that a mesh axis runs over, the one named last changes fastest.
Arguments:
- pair: float32 [256, 128, 128], P(('grp', 'row'), 'col'), parts along dimension 0, may hold values from -6 to 6
- mask: int32 [256], P('grp'), parts along dimension 0, may hold values from 0 to 1, as said below
- w_edges: bfloat16 [128, 4, 128], P(None, None, 'sub'), may hold values from -0.5 to 0.5
- w_outgate: bfloat16 [128, 128], replicated, may hold values from -0.5 to 0.5
- w_outproj: bfloat16 [128, 128], replicated, may hold values from -0.5 to 0.5
- w_attend: bfloat16 [128, 4, 128], P(None, None, 'sub'), may hold values from -0.5 to 0.5
- w_bias: bfloat16 [128, 4], P(None, 'sub'), may hold values from -16 to 16
- w_attout: bfloat16 [128, 128], P('sub'), may hold values from -0.5 to 0.5
Outputs:
- updated: float32 [256, 128, 128], P(('grp', 'row'), 'col'), parts along dimension 0
There are 2 independent parts, one for each index of `grp`. A program takes and returns all parts, laid end to end along the dimension named above; an argument that names none is the same for every part. Nothing has to cross between parts.
Inputs may be any that keep to these rules, and one draw needn't show every extreme that they name: mask is 1 for residues 0 to L-1 and 0 after, with L of 64 to 128.
All inputs are finite; a program needn't handle non-finite values.
Results may differ from a plain program's by a relative error of at most 0.025.
Values may be sent and summed in bfloat16 or wider, within the bound.
A program may use at most 64 MiB of HBM per device.

v0:
```python
import jax
import jax.numpy as jnp
from jax import lax
from jax.sharding import PartitionSpec as P

EPS = 1e-05


def layer_norm(values, axis):
    mean = jnp.mean(values, axis=axis, keepdims=True)
    centred = values - mean
    variance = jnp.mean(centred * centred, axis=axis, keepdims=True)
    return centred * lax.rsqrt(variance + EPS)


def body(pair, mask, w_edges, w_outgate, w_outproj, w_attend, w_bias, w_attout):
    rows, cols, channels = pair.shape
    row_start = lax.axis_index("row") * rows
    col_start = lax.axis_index("col") * cols
    mfloat = mask.astype(jnp.float32)
    mask_rows = lax.dynamic_slice_in_dim(mfloat, row_start, rows, 0)
    mask_cols = lax.dynamic_slice_in_dim(mfloat, col_start, cols, 0)
    pmask = mask_rows[:, None] * mask_cols[None, :]
    normed = layer_norm(pair, -1).astype(jnp.bfloat16)
    projected = jnp.einsum("ijc,cqh->qhij", normed, w_edges, preferred_element_type=jnp.float32)
    left = (pmask * jax.nn.sigmoid(projected[0]) * projected[1]).astype(jnp.bfloat16)
    right = (pmask * jax.nn.sigmoid(projected[2]) * projected[3]).astype(jnp.bfloat16)
    row_count = lax.axis_size("row")
    col_count = lax.axis_size("col")
    devices = row_count * col_count
    hidden = left.shape[0]
    if devices % hidden == 0:
        groups = 1
        copies = devices // hidden
    else:
        groups = hidden // devices
        copies = 1
    share = rows // copies
    left_send = left.reshape(devices, groups * share, cols)
    right_send = jnp.repeat(right, copies, axis=0).reshape(devices, groups, rows, cols)
    left_got, right_got = (
        lax.all_to_all(left_send, ("row", "col"), split_axis=0, concat_axis=0, tiled=True),
        lax.all_to_all(right_send, ("row", "col"), split_axis=0, concat_axis=0, tiled=True),
    )
    left_owned = left_got.reshape(row_count, col_count, groups, share, cols)
    left_owned = left_owned.transpose(2, 0, 3, 1, 4).reshape(
        groups, row_count * share, col_count * cols
    )
    right_owned = right_got.reshape(row_count, col_count, groups, rows, cols)
    right_owned = right_owned.transpose(2, 0, 3, 1, 4).reshape(
        groups, row_count * rows, col_count * cols
    )
    owned_sums = jnp.einsum(
        "gak,gjk->gaj", left_owned, right_owned, preferred_element_type=jnp.float32
    )
    outgoing = owned_sums.reshape(groups, row_count, share, col_count, cols)
    outgoing = outgoing.transpose(1, 3, 0, 2, 4).reshape(devices, groups * share, cols)
    returned = lax.all_to_all(outgoing, ("row", "col"), split_axis=0, concat_axis=0, tiled=True)
    edges = returned.reshape(hidden, rows, cols)
    all_edges = lax.all_gather(edges, "sub", axis=0, tiled=True)
    edgenorm = layer_norm(all_edges, 0).astype(jnp.bfloat16)
    outgate = jax.nn.sigmoid(
        jnp.einsum("ijc,cd->ijd", normed, w_outgate, preferred_element_type=jnp.float32)
    )
    first = pair + outgate * jnp.einsum(
        "hij,hd->ijd", edgenorm, w_outproj, preferred_element_type=jnp.float32
    )
    second = layer_norm(first, -1).astype(jnp.bfloat16)
    attproj = jnp.einsum("ijc,cqe->qije", second, w_attend, preferred_element_type=jnp.float32)
    query = attproj[0].astype(jnp.bfloat16)
    keyed = attproj[1].astype(jnp.bfloat16)
    valued = attproj[2].astype(jnp.bfloat16)
    attgate = attproj[3]
    bias = jnp.einsum("ijc,ch->hij", second, w_bias, preferred_element_type=jnp.float32).astype(
        jnp.bfloat16
    )
    all_keys, all_values = (
        lax.all_gather(keyed, "col", axis=1, tiled=True),
        lax.all_gather(valued, "col", axis=1, tiled=True),
    )
    bias_full = lax.all_gather(bias, "col", axis=2, tiled=True)
    bias_every = lax.all_gather(bias_full, "row", axis=1, tiled=True)
    bias_strip = lax.dynamic_slice_in_dim(bias_every, col_start, cols, 1)
    heads = w_bias.shape[1]
    width = query.shape[2]
    head_size = width // heads
    total = all_keys.shape[1]
    query_heads = query.reshape(rows, cols, heads, head_size)
    key_heads = all_keys.reshape(rows, total, heads, head_size)
    value_heads = all_values.reshape(rows, total, heads, head_size)
    maskbias = 1000000000.0 * (mfloat - 1.0)
    scores = jnp.einsum(
        "ijhd,ikhd->hijk", query_heads, key_heads, preferred_element_type=jnp.float32
    )
    scores = scores / jnp.sqrt(jnp.float32(head_size))
    scores = scores + bias_strip.astype(jnp.float32)[:, None, :, :] + maskbias[None, None, None, :]
    weights = jax.nn.softmax(scores, axis=-1).astype(jnp.bfloat16)
    attended = jnp.einsum(
        "hijk,ikhd->ijhd", weights, value_heads, preferred_element_type=jnp.float32
    )
    mixed = (attended.reshape(rows, cols, width) * jax.nn.sigmoid(attgate)).astype(jnp.bfloat16)
    terms = jnp.einsum("ije,ec->ijc", mixed, w_attout, preferred_element_type=jnp.float32)
    summed = lax.psum(terms.astype(jnp.bfloat16), "sub").astype(jnp.float32)
    return first + summed


def solution(mesh):
    placed = (
        P(("grp", "row"), "col", None),
        P("grp"),
        P(None, None, "sub"),
        P(),
        P(),
        P(None, None, "sub"),
        P(None, "sub"),
        P("sub", None),
    )
    return jax.shard_map(
        body, mesh=mesh, in_specs=placed, out_specs=P(("grp", "row"), "col", None), check_vma=False
    )
```

profile of v0, /device:TPU:0, one launch (start us, length us, event | category | flops | bytes accessed | tf_op | source)
XLA Modules:
  0.0 141.7 jit_solution(7199812480993205391)
XLA Ops:
  6.5 0.8 convert_element_type.57
  7.4 1.6 %reduce_sum.63 = f32[16,128]{1,0:T(8,128)S(1)} reduce(f32[16,128,128]{2,1,0:T(8,128)} %param.8, f32[]{:T(128)} %constant.14.clone.1), dimensions={2}, to_apply=%region_0.0 | reduce | flops 260096 | bytes 1056772 | tf_op jit(solution)/shard_map/reduce_sum | solution.py:10
  9.0 1.9 %multiply_reduce_fusion.2 = f32[16,128]{1,0:T(8,128)S(1)} fusion(f32[16,128,128]{2,1,0:T(8,128)} %param.8, f32[16,128]{1,0:T(8,128)S(1)} %broadcast_multiply_fusion.3), kind=kLoop, calls=%fused_computation.27 | loop fusion | flops 784384 | bytes 1064960 | tf_op jit(solution)/shard_map/reduce_sum | solution.py:12
  10.9 1.2 convolution_bitcast_fusion.1
  12.4 0.8 fusion.31
  13.2 7.2 %all-to-all-start.1 = ((bf16[8,8,16,128]{3,1,2,0:T(8,128)(2,1)}), bf16[8,8,16,128]{3,1,2,0:T(8,128)(2,1)S(1)}, u32[]{:S(2)}, u32[]{:S(2)}) async-start(bf16[8,8,16,128]{3,1,2,0:T(8,128)(2,1)} %fusion.31), calls=%async_computation.1 | async-start | bytes 524288 | tf_op jit(solution)/shard_map/all_to_all | solution.py:43
  21.1 0.8 fusion.28
  21.9 7.5 %all-to-all-done.1 = bf16[8,8,16,128]{3,1,2,0:T(8,128)(2,1)S(1)} async-done(((bf16[8,8,16,128]{3,1,2,0:T(8,128)(2,1)}), bf16[8,8,16,128]{3,1,2,0:T(8,128)(2,1)S(1)}, u32[]{:S(2)}, u32[]{:S(2)}) %all-to-all-start.1) | async-done | bytes 262176 | tf_op jit(solution)/shard_map/all_to_all | solution.py:43
  29.3 3.6 %all-to-all-start = ((bf16[8,128,128]{2,1,0:T(8,128)(2,1)}), bf16[8,128,128]{2,1,0:T(8,128)(2,1)S(1)}, u32[]{:S(2)}, u32[]{:S(2)}) async-start(bf16[8,128,128]{2,1,0:T(8,128)(2,1)} %fusion.28), calls=%async_computation | async-start | bytes 524288 | tf_op jit(solution)/shard_map/all_to_all | solution.py:42
  33.0 8.5 %all-to-all-done = bf16[8,128,128]{2,1,0:T(8,128)(2,1)S(1)} async-done(((bf16[8,128,128]{2,1,0:T(8,128)(2,1)}), bf16[8,128,128]{2,1,0:T(8,128)(2,1)S(1)}, u32[]{:S(2)}, u32[]{:S(2)}) %all-to-all-start) | async-done | bytes 262176 | tf_op jit(solution)/shard_map/all_to_all | solution.py:42
  41.9 17.5 %all_to_all.15 = f32[8,128,128]{2,1,0:T(8,128)} all-to-all(f32[8,128,128]{2,1,0:T(8,128)S(1)} %bitcast.90), channel_id=1, replica_groups=mesh['grp'=2,'row'=8,'col'=1,'sub'=2] {'row','col'}, dimensions={0} | all-to-all | bytes 1048576 | tf_op jit(solution)/shard_map/all_to_all | solution.py:58
  59.8 7.9 %all-gather.2.cloned.1.call-done = f32[128,16,128]{2,1,0:T(8,128)} async-done(((f32[64,16,128]{2,1,0:T(8,128)}), f32[128,16,128]{2,1,0:T(8,128)}) %all-gather.2.cloned.1.call-update) | async-done | bytes 1048592 | tf_op jit(solution)/shard_map/all_gather | solution.py:60
  67.7 1.5 %reduce_sum.65 = f32[16,128]{1,0:T(8,128)S(1)} reduce(f32[128,16,128]{2,1,0:T(8,128)} %all-gather.2.cloned.1.call-done, f32[]{:T(128)} %constant.14.clone.1), dimensions={0}, to_apply=%region_2.0 | reduce | flops 260096 | bytes 1056772 | tf_op jit(solution)/shard_map/reduce_sum | solution.py:10
  69.1 1.4 multiply_reduce_fusion.1
  71.1 1.8 %fusion.56 = (f32[16,128]{1,0:T(8,128)S(1)}, f32[16,128,128]{1,2,0:T(8,128)S(1)}) fusion(f32[16,128,128]{1,2,0:T(8,128)S(1)} %copy.67, f32[16,128,128]{1,2,0:T(8,128)S(1)} %fusion.29, bf16[128,128]{1,0:T(8,128)(2,1)S(1)} %copy-done.7, f32[16,128,128]{2,1,0:T(8,128)S(1)} %copy-done.1, f32[16,128]{1,0:T(8,128)S(1)} %add_rsqrt_fusion.2, ...), kind=kOutput, calls=%fused_computation.75 | convolution fusion | flops 69466112 | bytes 4251648 | tf_op jit(solution)/shard_map/ijc,cd->ijd/dot_general | solution.py:63
  73.3 30.8 %all_gather.10 = bf16[2,128,128]{2,0,1:T(2,128)(2,1)S(1)} all-gather(bf16[2,16,128]{2,0,1:T(2,128)(2,1)S(1)} %fusion.7), channel_id=1, replica_groups=mesh['grp'=2,'row'=8,'col'=1,'sub'=2] {'row'}, dimensions={1}, use_global_device_ids=true | all-gather | bytes 73728 | tf_op jit(solution)/shard_map/all_gather | solution.py:82
  104.2 1.8 %fusion.57 = (bf16[4,16,128,64]{2,3,0,1:T(8,128)(2,1)S(1)}, f32[4,16,128,64]{2,3,0,1:T(8,128)}) fusion(bf16[128,4,64]{0,2,1:T(8,128)(2,1)S(1)} %copy-done, f32[16,128]{1,0:T(8,128)S(1)} %add_rsqrt_fusion, f32[16,128,128]{1,2,0:T(8,128)S(1)} %get-tuple-element.13, f32[16,128]{1,0:T(8,128)S(1)} %broadcast_multiply_fusion.1), kind=kOutput, calls=%fused_computation.76 | convolution fusion | flops 135528448 | bytes 4276224 | tf_op jit(solution)/shard_map/ijc,cqe->qije/dot_general | solution.py:69
  106.1 2.2 %fusion.58 = (f32[2,16,128]{2,1,0:T(8,128)S(1)}, f32[2,16,128,128]{2,3,1,0:T(8,128)}) fusion(f32[128]{0:T(128)S(1)} %add_multiply_fusion, f32[2,128,128]{1,2,0:T(8,128)S(1)} %copy.73, bf16[16,128,2,32]{1,3,2,0:T(8,128)(2,1)S(1)} %bitcast.97, bf16[16,128,2,32]{1,3,2,0:T(8,128)(2,1)S(1)} %bitcast.96), kind=kOutput, calls=%fused_computation.77 | convolution fusion | flops 36176000 | bytes 2769408 | tf_op jit(solution)/shard_map/sub | solution.py:97
  108.3 2.0 %fusion.8 = f32[16,2,32,128]{3,2,1,0:T(8,128)S(1)} fusion(bf16[16,128,2,32]{1,3,2,0:T(8,128)(2,1)S(1)} %bitcast.95, f32[2,16,128,128]{2,3,1,0:T(8,128)} %get-tuple-element.17, f32[2,16,128]{2,1,0:T(8,128)S(1)} %get-tuple-element.16), kind=kOutput, calls=%fused_computation.16 | convolution fusion | flops 34603008 | bytes 2899968 | tf_op jit(solution)/shard_map/hijk,ikhd->ijhd/dot_general | solution.py:98
  110.3 1.2 fusion.32
  111.5 1.1 convolution_convert_fusion
  112.6 19.7 %all-reduce.2.cloned.1.call-done = bf16[16,128,128]{1,2,0:T(8,128)(2,1)} async-done(((bf16[16,128,128]{1,2,0:T(8,128)(2,1)}), bf16[16,128,128]{1,2,0:T(8,128)(2,1)}) %all-reduce.2.cloned.1.call-update) | async-done | bytes 524304 | tf_op jit(solution)/shard_map/psum | solution.py:103
  132.4 1.1 convert_add_fusion
  133.5 1.3 copy.76
  (47 shorter events, 3.0 us)
Async XLA Ops:
  6.5 97.6 %copy-start = (bf16[128,4,64]{0,2,1:T(8,128)(2,1)S(1)}, bf16[128,4,64]{0,2,1:T(8,128)(2,1)}, u32[]{:S(2)}) copy-start(bf16[128,4,64]{0,2,1:T(8,128)(2,1)} %param.13) | copy-start | bytes 196612
  6.5 4.4 %copy-start.1 = (f32[16,128,128]{2,1,0:T(8,128)S(1)}, f32[16,128,128]{2,1,0:T(8,128)}, u32[]{:S(2)}) copy-start(f32[16,128,128]{2,1,0:T(8,128)} %param.8) | copy-start | bytes 3145732
  6.5 4.4 %copy-start.3 = (bf16[128,4,64]{0,2,1:T(8,128)(2,1)S(1)}, bf16[128,4,64]{0,2,1:T(8,128)(2,1)}, u32[]{:S(2)}) copy-start(bf16[128,4,64]{0,2,1:T(8,128)(2,1)} %param.10) | copy-start | bytes 196612
  13.2 16.2 %all-to-all-start.1 = ((bf16[8,8,16,128]{3,1,2,0:T(8,128)(2,1)}), bf16[8,8,16,128]{3,1,2,0:T(8,128)(2,1)S(1)}, u32[]{:S(2)}, u32[]{:S(2)}) async-start(bf16[8,8,16,128]{3,1,2,0:T(8,128)(2,1)} %fusion.31), calls=%async_computation.1 | async-start | bytes 524288 | tf_op jit(solution)/shard_map/all_to_all | solution.py:43
  29.3 12.2 %all-to-all-start = ((bf16[8,128,128]{2,1,0:T(8,128)(2,1)}), bf16[8,128,128]{2,1,0:T(8,128)(2,1)S(1)}, u32[]{:S(2)}, u32[]{:S(2)}) async-start(bf16[8,128,128]{2,1,0:T(8,128)(2,1)} %fusion.28), calls=%async_computation | async-start | bytes 524288 | tf_op jit(solution)/shard_map/all_to_all | solution.py:42
  32.9 34.7 %all-gather.2.cloned.1.call-start = ((), (), s32[]{:S(2)}) async-start(), calls=%async_computation.3 | async-start | bytes 1572864 | tf_op jit(solution)/shard_map/all_gather | solution.py:60
  41.9 17.9 %copy-start.8 = (s32[128]{0:T(128)S(1)}, s32[128]{0:T(128)}, u32[]{:S(2)}) copy-start(s32[128]{0:T(128)} %param.9) | copy-start | bytes 1540
  59.4 73.0 %all-reduce.2.cloned.1.call-start = ((), (), s32[]{:S(2)}) async-start(), calls=%async_computation.4 | async-start | bytes 1048576 | tf_op jit(solution)/shard_map/psum | solution.py:103
  59.8 10.9 %copy-start.4 = (bf16[128,128]{1,0:T(8,128)(2,1)S(1)}, bf16[128,128]{1,0:T(8,128)(2,1)}, u32[]{:S(2)}) copy-start(bf16[128,128]{1,0:T(8,128)(2,1)} %param.12) | copy-start | bytes 98308
  67.7 2.9 %copy-start.2 = (f32[128,16,128]{2,1,0:T(8,128)S(1)}, f32[128,16,128]{2,1,0:T(8,128)}, u32[]{:S(2)}) copy-start(f32[128,16,128]{2,1,0:T(8,128)} %all-gather.2.cloned.1.call-done) | copy-start | bytes 3145732
  69.1 1.9 %copy-start.7 = (bf16[128,128]{1,0:T(8,128)(2,1)S(1)}, bf16[128,128]{1,0:T(8,128)(2,1)}, u32[]{:S(2)}) copy-start(bf16[128,128]{1,0:T(8,128)(2,1)} %param.11) | copy-start | bytes 98308
  71.0 2.0 %copy-start.6 = (bf16[128,2]{0,1:T(2,128)(2,1)S(1)}, bf16[128,2]{0,1:T(2,128)(2,1)}, u32[]{:S(2)}) copy-start(bf16[128,2]{0,1:T(2,128)(2,1)} %param.14) | copy-start | bytes 1540
  108.3 3.2 %copy-start.5 = (bf16[64,128]{1,0:T(8,128)(2,1)S(1)}, bf16[64,128]{1,0:T(8,128)(2,1)}, u32[]{:S(2)}) copy-start(bf16[64,128]{1,0:T(8,128)(2,1)} %param.15) | copy-start | bytes 49156
Sparse Core Ops, SparseCore 0:
  59.5 8.1 all-gather.1
  112.8 19.5 all-reduce.1
where the time goes:
time: 142 us
  blocking collectives  48.3 us (34%)
  waiting for transfers between devices  43.6 us (31%)
  between operations  13.7 us (10%)
  other arithmetic  11.6 us (8%)
  matrix products  11 us (8%)
  starting transfers between devices  10.9 us (8%)
  local copies, waits for them, and re-layouts  2.66 us (2%)
    all_gather x1, blocking collectives, body(): bias_every = lax.all_gather(bias_full, 'row', axis=1, tiled=True)  30.8 us
    psum x1, waiting for transfers between devices, body(): summed = lax.psum(terms.astype(jnp.bfloat16), 'sub').astype(jnp.float32)  19.7 us
    all_to_all x1, blocking collectives, body(): lax.all_to_all(outgoing, ('row', 'col'), split_axis=0, concat_axis=0, til...  17.5 us
    all_to_all x1, waiting for transfers between devices, body(): lax.all_to_all(left_send, ('row', 'col'), split_axis=0, concat_axis=0, ti...  8.48 us
    all_gather x1, waiting for transfers between devices, body(): all_edges = lax.all_gather(edges, 'sub', axis=0, tiled=True)  7.85 us
    all_to_all x1, waiting for transfers between devices, body(): lax.all_to_all(right_send, ('row', 'col'), split_axis=0, concat_axis=0, t...  7.47 us
    all_to_all x1, starting transfers between devices, body(): lax.all_to_all(right_send, ('row', 'col'), split_axis=0, concat_axis=0, t...  7.25 us
    all_to_all x1, starting transfers between devices, body(): lax.all_to_all(left_send, ('row', 'col'), split_axis=0, concat_axis=0, ti...  3.59 us
  transfers between devices with their start and end apart: 4, of which 4 were waited for; matrix products, arithmetic and copies ran while one was open for 1% of the time, Pallas kernels for 0%

commit v1 on v0

--- a/solution.py
+++ b/solution.py
@@ -1,9 +1,310 @@
 import jax
 import jax.numpy as jnp
 from jax import lax
+from jax.experimental import pallas as pl
+from jax.experimental.pallas import tpu as pltpu
 from jax.sharding import PartitionSpec as P
 
 EPS = 1e-05
+MESH = pl.DeviceIdType.MESH
+CHUNKS = 4
+
+
+def dot(a, b):
+    return jnp.dot(a, b, preferred_element_type=jnp.float32)
+
+
+def norm_rows(values):
+    mean = jnp.mean(values, axis=0, keepdims=True)
+    centred = values - mean
+    variance = jnp.mean(centred * centred, axis=0, keepdims=True)
+    return centred * lax.rsqrt(variance + EPS)
+
+
+def turned(ref_value):
+    return ref_value.astype(jnp.float32).T
+
+
+def fused_kernel(
+    pair_ref, mask_ref, smask_ref, we_ref, wog_ref, wop_ref, wa_ref, wb_ref, wo_ref,
+    out_ref,
+    wet, wa_all, wb_all, wo_all, sent, got, wide, pair_t, normed_t, gates, back, owned, wide2,
+    first_t, second_t, bias_rows, bias_send, bias_got, bias_t, query_t, keyed, value_t, attgate_t,
+    w_send, w_recv, a_send, a_recv, b_send, b_recv, c_send, c_recv, o_send, o_recv,
+):
+    row = lax.axis_index("row")
+    sub = lax.axis_index("sub")
+    other = 1 - sub
+    count = 8
+    rows = 16
+    half = 8
+    step = rows // CHUNKS
+
+    def at_row(offset):
+        return lax.rem(row + offset, count)
+
+    def from_row(offset):
+        return lax.rem(row + count - offset, count)
+
+    barrier = pltpu.get_barrier_semaphore()
+    peers = [(o, d) for o in range(count) for d in range(2) if (o, d) != (0, 0)]
+
+    def peer_sub(d):
+        return sub if d == 0 else other
+
+    for o, d in peers:
+        pl.semaphore_signal(
+            barrier, inc=1, device_id={"row": at_row(o), "sub": peer_sub(d)}, device_id_type=MESH
+        )
+
+    turned_we = turned(we_ref[...])
+    gate_rows = [turned_we[128 * lr + 8 * p:128 * lr + 8 * p + 8] for p in range(8) for lr in range(2)]
+    value_rows = [
+        turned_we[128 * lr + 64 + 8 * p:128 * lr + 64 + 8 * p + 8] for p in range(8) for lr in range(2)
+    ]
+    wet[...] = jnp.concatenate(gate_rows + value_rows, axis=0).astype(jnp.bfloat16)
+    mask_lanes = mask_ref[...].astype(jnp.float32)
+
+    def edge_row(i, carry):
+        x = pair_ref[i].T
+        pair_t[i] = x
+        normed = norm_rows(x).astype(jnp.bfloat16)
+        normed_t[i] = normed
+        projected = dot(wet[...], normed)
+        mask_row = smask_ref[row * rows + i].astype(jnp.float32)
+        edge = (mask_lanes * mask_row) * jax.nn.sigmoid(projected[:128]) * projected[128:]
+        edge = edge.astype(jnp.bfloat16)
+        for p in range(8):
+            sent[p, i] = edge[16 * p:16 * p + 16]
+        return carry
+
+    def a_copy(o, c, slot_from, slot_to):
+        part = pl.ds(c * step, step)
+        return pltpu.make_async_remote_copy(
+            src_ref=sent.at[slot_from, part],
+            dst_ref=got.at[slot_to, part],
+            send_sem=a_send.at[o, c],
+            recv_sem=a_recv.at[o, c],
+            device_id={"row": at_row(o)},
+            device_id_type=MESH,
+        )
+
+    def w_copy(k, src, dst):
+        return pltpu.make_async_remote_copy(
+            src_ref=src, dst_ref=dst, send_sem=w_send.at[k], recv_sem=w_recv.at[k],
+            device_id={"sub": other}, device_id_type=MESH,
+        )
+
+    order = [4, 3, 5, 2, 6, 1, 7]
+    for c in range(CHUNKS):
+        lax.fori_loop(c * step, (c + 1) * step, edge_row, 0, unroll=2)
+        if c == 0:
+            pl.semaphore_wait(barrier, len(peers))
+        for o in order:
+            a_copy(o, c, at_row(o), row).start()
+    for k, (src, dst) in enumerate(((wa_ref, wa_all), (wb_ref, wb_all), (wo_ref, wo_all))):
+        w_copy(k, src, dst.at[sub]).start()
+
+    wa_all[sub] = wa_ref[...]
+    wb_all[sub] = wb_ref[...]
+    wo_all[sub] = wo_ref[...]
+    outgate_t = turned(wog_ref[...]).astype(jnp.bfloat16)
+
+    def gate_row(i, carry):
+        gates[i] = jax.nn.sigmoid(dot(outgate_t, normed_t[sub * half + i]))
+        return carry
+
+    lax.fori_loop(0, half, gate_row, 0, unroll=2)
+    outproj_t = turned(wop_ref[...]).astype(jnp.bfloat16)
+
+    wide[pl.ds(pl.multiple_of(row * 256, 256), 256), :] = (
+        sent[row].reshape(256, 128).astype(jnp.float32)
+    )
+    for o in order[::-1]:
+        source = from_row(o)
+        for c in range(CHUNKS):
+            a_copy(o, c, source, source).wait_recv()
+        wide[pl.ds(pl.multiple_of(source * 256, 256), 256), :] = (
+            got[source].reshape(256, 128).astype(jnp.float32)
+        )
+
+    for pair_of in range(4):
+        sums = []
+        for h in (2 * pair_of, 2 * pair_of + 1):
+            left = wide[pl.ds(h, 128, stride=16), :].astype(jnp.bfloat16)
+            right = wide[pl.ds(8 + h, 128, stride=16), :].astype(jnp.bfloat16)
+            total = lax.dot_general(
+                left, right, (((1,), (1,)), ((), ())), preferred_element_type=jnp.float32
+            )
+            sums.append(total.reshape(16, 8, 128))
+        back[:, pl.ds(16 * pair_of, 16), :] = jnp.concatenate(sums, axis=1).astype(jnp.bfloat16)
+
+    def b_copy(k, o, d, src, dst):
+        return pltpu.make_async_remote_copy(
+            src_ref=back.at[src], dst_ref=owned.at[dst], send_sem=b_send.at[k], recv_sem=b_recv.at[k],
+            device_id={"row": at_row(o), "sub": peer_sub(d)}, device_id_type=MESH,
+        )
+
+    ranked = [(o, d) for o in order for d in (1, 0)] + [(0, 1)]
+    for k, (o, d) in enumerate(ranked):
+        b_copy(k, o, d, at_row(o) * 2 + peer_sub(d), sub * 8 + row).start()
+    wide2[pl.ds(pl.multiple_of((sub * 8 + row) * 64, 64), 64), :] = (
+        back[row * 2 + sub].astype(jnp.float32)
+    )
+
+    for k, (src, dst) in enumerate(((wa_ref, wa_all), (wb_ref, wb_all), (wo_ref, wo_all))):
+        w_copy(k, src, dst.at[other]).wait_recv()
+    wat = [turned(wa_all[s]).astype(jnp.bfloat16) for s in range(2)]
+    attend_t = jnp.concatenate(
+        [wat[s][64 * q:64 * q + 64] for q in range(4) for s in range(2)], axis=0
+    )
+    bias_w = wb_all[...].reshape(32, 128)
+    attout_t = turned(wo_all[...].reshape(128, 128)).astype(jnp.bfloat16)
+
+    for k in reversed(range(len(ranked))):
+        o, d = ranked[k]
+        source = peer_sub(d) * 8 + from_row(o)
+        b_copy(k, o, d, 0, source).wait_recv()
+        wide2[pl.ds(pl.multiple_of(source * 64, 64), 64), :] = owned[source].astype(jnp.float32)
+
+    for i in range(half):
+        edgenorm = norm_rows(wide2[pl.ds(i, 128, stride=8), :]).astype(jnp.bfloat16)
+        first = pair_t[sub * half + i] + gates[i] * dot(outproj_t, edgenorm)
+        first_t[i] = first
+        second = norm_rows(first).astype(jnp.bfloat16)
+        second_t[i] = second
+        bias = dot(bias_w, second)
+        for n in range(4):
+            r = 16 * (n // 2) + n % 2
+            bias_rows[n * 8 + i:n * 8 + i + 1, :] = bias[r:r + 1]
+    bias_send[...] = bias_rows[...].astype(jnp.bfloat16)
+
+    def c_copy(k, o, d, dst):
+        return pltpu.make_async_remote_copy(
+            src_ref=bias_send, dst_ref=bias_got.at[dst], send_sem=c_send.at[k], recv_sem=c_recv.at[k],
+            device_id={"row": at_row(o), "sub": peer_sub(d)}, device_id_type=MESH,
+        )
+
+    for k, (o, d) in enumerate(ranked):
+        c_copy(k, o, d, row * 2 + sub).start()
+
+    def project_row(i, carry):
+        projected = dot(attend_t, second_t[i])
+        query_t[i] = projected[:128].astype(jnp.bfloat16)
+        keyed[i] = projected[128:256].T.astype(jnp.bfloat16)
+        value_t[i] = projected[256:384].astype(jnp.bfloat16)
+        attgate_t[i] = jax.nn.sigmoid(projected[384:])
+        return carry
+
+    lax.fori_loop(0, half, project_row, 0, unroll=2)
+
+    mine = row * 2 + sub
+    bias_got[mine] = bias_send[...]
+    for k in reversed(range(len(ranked))):
+        o, d = ranked[k]
+        c_copy(k, o, d, from_row(o) * 2 + peer_sub(d)).wait_recv()
+    maskbias = 1000000000.0 * (mask_lanes - 1.0)
+    all_bias = bias_got[...].astype(jnp.float32)
+    for n in range(4):
+        bias_t[n] = (all_bias[:, n * 8:n * 8 + 8, :].reshape(128, 128) + maskbias).T
+
+    scale = 1.0 / (32.0 ** 0.5)
+
+    def o_copy(i, at):
+        return pltpu.make_async_remote_copy(
+            src_ref=out_ref.at[at * half + i], dst_ref=out_ref.at[at * half + i],
+            send_sem=o_send.at[i], recv_sem=o_recv.at[i],
+            device_id={"sub": other}, device_id_type=MESH,
+        )
+
+    def attend_row(i, carry):
+        query = query_t[i]
+        key = keyed[i]
+        value = value_t[i]
+        nothing = jnp.zeros((32, 128), jnp.bfloat16)
+        mixed = []
+        for n in range(4):
+            head = jnp.concatenate(
+                [query[32 * m:32 * m + 32] if m == n else nothing for m in range(4)], axis=0
+            )
+            scores = dot(key, head) * scale + bias_t[n]
+            top = jnp.max(scores, axis=0, keepdims=True)
+            weights = jnp.exp(scores - top)
+            total = jnp.sum(weights, axis=0, keepdims=True)
+            mixed.append(dot(value[32 * n:32 * n + 32], weights.astype(jnp.bfloat16)) / total)
+        mixed = (jnp.concatenate(mixed, axis=0) * attgate_t[i]).astype(jnp.bfloat16)
+        out_ref[sub * half + i] = (first_t[i] + dot(attout_t, mixed)).T
+        o_copy(i, sub).start()
+        return carry
+
+    lax.fori_loop(0, half, attend_row, 0, unroll=2)
+
+    for k, (src, dst) in enumerate(((wa_ref, wa_all), (wb_ref, wb_all), (wo_ref, wo_all))):
+        w_copy(k, src, dst.at[sub]).wait_send()
+    for c in range(CHUNKS):
+        for o in order:
+            a_copy(o, c, at_row(o), row).wait_send()
+    for k, (o, d) in enumerate(ranked):
+        b_copy(k, o, d, at_row(o) * 2 + peer_sub(d), sub * 8 + row).wait_send()
+        c_copy(k, o, d, row * 2 + sub).wait_send()
+    for i in range(half):
+        o_copy(i, sub).wait_send()
+        o_copy(i, other).wait_recv()
+
+
+def fused_body(pair, mask, w_edges, w_outgate, w_outproj, w_attend, w_bias, w_attout):
+    f32, bf16 = jnp.float32, jnp.bfloat16
+    vmem = pl.BlockSpec(memory_space=pltpu.VMEM)
+    bias_rows = jnp.pad(w_bias.T, ((0, 14), (0, 0)))
+    dma = pltpu.SemaphoreType.DMA
+    return pl.pallas_call(
+        fused_kernel,
+        out_shape=jax.ShapeDtypeStruct(pair.shape, f32),
+        in_specs=[vmem, vmem, pl.BlockSpec(memory_space=pltpu.SMEM)] + [vmem] * 6,
+        out_specs=vmem,
+        scratch_shapes=[
+            pltpu.VMEM((256, 128), bf16),
+            pltpu.VMEM((2, 128, 256), bf16),
+            pltpu.VMEM((2, 16, 128), bf16),
+            pltpu.VMEM((2, 64, 128), bf16),
+            pltpu.VMEM((8, 16, 16, 128), bf16),
+            pltpu.VMEM((8, 16, 16, 128), bf16),
+            pltpu.VMEM((2048, 128), f32),
+            pltpu.VMEM((16, 128, 128), f32),
+            pltpu.VMEM((16, 128, 128), bf16),
+            pltpu.VMEM((8, 128, 128), f32),
+            pltpu.VMEM((16, 64, 128), bf16),
+            pltpu.VMEM((16, 64, 128), bf16),
+            pltpu.VMEM((1024, 128), f32),
+            pltpu.VMEM((8, 128, 128), f32),
+            pltpu.VMEM((8, 128, 128), bf16),
+            pltpu.VMEM((32, 128), f32),
+            pltpu.VMEM((32, 128), bf16),
+            pltpu.VMEM((16, 32, 128), bf16),
+            pltpu.VMEM((4, 128, 128), f32),
+            pltpu.VMEM((8, 128, 128), bf16),
+            pltpu.VMEM((8, 128, 128), bf16),
+            pltpu.VMEM((8, 128, 128), bf16),
+            pltpu.VMEM((8, 128, 128), f32),
+            dma((3,)), dma((3,)),
+            dma((8, CHUNKS)), dma((8, CHUNKS)),
+            dma((15,)), dma((15,)),
+            dma((15,)), dma((15,)),
+            dma((8,)), dma((8,)),
+        ],
+        compiler_params=pltpu.CompilerParams(
+            collective_id=0, has_side_effects=True, vmem_limit_bytes=40 * 1024 * 1024
+        ),
+        name="window",
+    )(
+        pair, mask.reshape(1, 128), mask, w_edges.reshape(128, 256), w_outgate, w_outproj,
+        w_attend.reshape(128, 256), bias_rows, w_attout,
+    )
+
+
+def fits(mesh):
+    sizes = dict(mesh.shape)
+    return sizes["col"] == 1 and sizes["row"] == 8 and sizes["sub"] == 2
 
 
 def layer_norm(values, axis):
@@ -115,6 +416,22 @@
         P(None, "sub"),
         P("sub", None),
     )
-    return jax.shard_map(
+    whole = jax.shard_map(
         body, mesh=mesh, in_specs=placed, out_specs=P(("grp", "row"), "col", None), check_vma=False
     )
+    if not fits(mesh):
+        return whole
+    fused = jax.shard_map(
+        fused_body, mesh=mesh, in_specs=placed, out_specs=P(("grp", "row"), "col", None), check_vma=False
+    )
+    parts = mesh.shape["grp"]
+    shapes = [
+        (128 * parts, 128, 128), (128 * parts,), (128, 4, 128), (128, 128), (128, 128), (128, 4, 128),
+        (128, 4), (128, 128),
+    ]
+
+    def run(*arrays):
+        same = [a.shape for a in arrays] == shapes
+        return (fused if same else whole)(*arrays)
+
+    return run

time: 142 us -> 45.1 us (0.32)
  blocking collectives: 48.3 us -> 0 us
  waiting for transfers between devices: 43.6 us -> 0 us
  Pallas kernels: 0 us -> 40.1 us
  between operations: 13.7 us -> 0.07 us
  other arithmetic: 11.6 us -> 0 us
  matrix products: 11 us -> 0 us
  starting transfers between devices: 10.9 us -> 0 us
  local copies, waits for them, and re-layouts: 2.66 us -> 4.57 us
    pallas_call x0 -> x1, Pallas kernels: none -> 40.1 us  [fused_body(): pl.pallas_call(fused_kernel, out_shape=jax.ShapeDtypeStruct(pair.shape, f...]
    all_gather x1 -> x0, blocking collectives: 30.8 us -> none  [body(): bias_every = lax.all_gather(bias_full, 'row', axis=1, tiled=True)]
    psum x1 -> x0, waiting for transfers between devices: 19.7 us -> none  [body(): summed = lax.psum(terms.astype(jnp.bfloat16), 'sub').astype(jnp.float32)]
    all_to_all x1 -> x0, blocking collectives: 17.5 us -> none  [body(): lax.all_to_all(outgoing, ('row', 'col'), split_axis=0, concat_axis=0, til...]
    all_to_all x2 -> x0, waiting for transfers between devices: 15.9 us -> none  [the longest x1 8.48 us: body(): lax.all_to_all(left_send, ('row', 'col'), split_axis=0, concat_axis=0, ti...]
    all_to_all x2 -> x0, starting transfers between devices: 10.8 us -> none  [the longest x1 7.25 us: body(): lax.all_to_all(right_send, ('row', 'col'), split_axis=0, concat_axis=0, t...]
    dot_general x8 -> x0, matrix products: 8.78 us -> none  [the longest x1 1.99 us: body(): jnp.einsum('hijk,ikhd->ijhd', weights, value_heads, preferred_element_typ...]
    all_gather x1 -> x0, waiting for transfers between devices: 7.85 us -> none  [body(): all_edges = lax.all_gather(edges, 'sub', axis=0, tiled=True)]
  transfers between devices with their start and end apart: 4 -> 0, of which waited for: 4 -> 0; matrix products, arithmetic and copies ran while one was open for 1% -> 0% of each run, Pallas kernels for 0% -> 0%
where the time goes in v1:
time: 45.1 us; the launch traced here: 44.8 us
  Pallas kernels  40.1 us (89%)
  local copies, waits for them, and re-layouts  4.57 us (10%)
    pallas_call x1, Pallas kernels, fused_body(): pl.pallas_call(fused_kernel, out_shape=jax.ShapeDtypeStruct(pair.shape, f...  40.1 us
    unnamed x15, local copies, waits for them, and re-layouts  3.49 us
    reshape x1, local copies, waits for them, and re-layouts, fused_body(): w_edges.reshape(128, 256)  0.97 us

profile of v1, /device:TPU:0, one launch (start us, length us, event | category | flops | bytes accessed | tf_op | source)
XLA Modules:
  0.0 44.8 jit_solution(10778618838462025638)
XLA Ops:
  0.0 0.0 copy-start.6
  0.0 0.7 %copy-done.6 = bf16[128,2]{0,1:T(2,128)(2,1)S(1)} copy-done((bf16[128,2]{0,1:T(2,128)(2,1)S(1)}, bf16[128,2]{0,1:T(2,128)(2,1)}, u32[]{:S(2)}) %copy-start.6) | copy-done | bytes 536
  0.7 0.0 copy-start.5
  0.7 1.0 %copy.11.we_ref = bf16[128,256]{1,0:T(8,128)(2,1)S(1)} copy(bf16[128,256]{0,1:T(8,128)(2,1)} %bitcast.5) | data formatting | bytes 131072 | tf_op jit(solution)/shard_map/reshape | solution.py:300
  1.6 0.0 copy-done.5
  1.6 0.0 copy-start.1
  1.7 0.0 copy-start.2
  1.7 0.0 copy-start.3
  1.7 0.0 copy-start.4
  1.7 0.1 copy.12.wa_ref
  1.8 0.6 %copy-done.1 = bf16[128,128]{1,0:T(8,128)(2,1)S(1)} copy-done((bf16[128,128]{1,0:T(8,128)(2,1)S(1)}, bf16[128,128]{1,0:T(8,128)(2,1)}, u32[]{:S(2)}) %copy-start.1) | copy-done | bytes 32792
  2.4 0.0 copy-done.2
  2.4 0.0 copy-done.3
  2.4 0.0 copy-done.4
  2.4 0.0 copy-start
  2.4 1.2 %copy-done = f32[16,128,128]{2,1,0:T(8,128)S(1)} copy-done((f32[16,128,128]{2,1,0:T(8,128)S(1)}, f32[16,128,128]{2,1,0:T(8,128)}, u32[]{:S(2)}) %copy-start) | copy-done | bytes 1048600
  3.7 40.1 %window.1 = f32[16,128,128]{2,1,0:T(8,128)S(1)} custom-call(f32[16,128,128]{2,1,0:T(8,128)S(1)} %copy-done, s32[1,128]{1,0:T(1,128)S(1)} %bitcast.4, s32[128]{0:T(128)S(1)} %copy-done.4, bf16[128,256]{1,0:T(8,128)(2,1)S(1)} %copy.11.we_ref, bf16[128,128]{1,0:T(8,128)(2,1)S(1)} %copy-done.1, bf16[128,128]{1,0:T(8,128)(2,1)S(1)} %copy-done.2, ...), custom_call_target="tpu_custom_call" | custom-call | tf_op jit(solution)/shard_map/window/pallas_call | solution.py:260
  43.8 1.0 %copy.14 = f32[16,128,128]{2,1,0:T(8,128)} copy(f32[16,128,128]{2,1,0:T(8,128)S(1)} %window.1) | data formatting | bytes 2097152
  (1 shorter events, 0.0 us)
Async XLA Ops:
  0.0 0.7 %copy-start.6 = (bf16[128,2]{0,1:T(2,128)(2,1)S(1)}, bf16[128,2]{0,1:T(2,128)(2,1)}, u32[]{:S(2)}) copy-start(bf16[128,2]{0,1:T(2,128)(2,1)} %param.14) | copy-start | bytes 1540
  0.7 1.0 %copy-start.5 = (bf16[128,4,64]{0,2,1:T(8,128)(2,1)S(1)}, bf16[128,4,64]{0,2,1:T(8,128)(2,1)}, u32[]{:S(2)}) copy-start(bf16[128,4,64]{0,2,1:T(8,128)(2,1)} %param.13) | copy-start | bytes 196612
  1.6 0.8 %copy-start.1 = (bf16[128,128]{1,0:T(8,128)(2,1)S(1)}, bf16[128,128]{1,0:T(8,128)(2,1)}, u32[]{:S(2)}) copy-start(bf16[128,128]{1,0:T(8,128)(2,1)} %wog_ref.1) | copy-start | bytes 98308
  1.7 0.8 %copy-start.2 = (bf16[128,128]{1,0:T(8,128)(2,1)S(1)}, bf16[128,128]{1,0:T(8,128)(2,1)}, u32[]{:S(2)}) copy-start(bf16[128,128]{1,0:T(8,128)(2,1)} %wop_ref.1) | copy-start | bytes 98308
  1.7 0.8 %copy-start.3 = (bf16[64,128]{1,0:T(8,128)(2,1)S(1)}, bf16[64,128]{1,0:T(8,128)(2,1)}, u32[]{:S(2)}) copy-start(bf16[64,128]{1,0:T(8,128)(2,1)} %wo_ref.1) | copy-start | bytes 49156
  1.7 0.7 %copy-start.4 = (s32[128]{0:T(128)S(1)}, s32[128]{0:T(128)}, u32[]{:S(2)}) copy-start(s32[128]{0:T(128)} %smask_ref.1) | copy-start | bytes 1540
  2.4 1.2 %copy-start = (f32[16,128,128]{2,1,0:T(8,128)S(1)}, f32[16,128,128]{2,1,0:T(8,128)}, u32[]{:S(2)}) copy-start(f32[16,128,128]{2,1,0:T(8,128)} %pair_ref.1) | copy-start | bytes 3145732

commit v2 on v1

--- a/solution.py
+++ b/solution.py
@@ -26,146 +26,173 @@
 
 
 def fused_kernel(
-    pair_ref, mask_ref, smask_ref, we_ref, wog_ref, wop_ref, wa_ref, wb_ref, wo_ref,
+    pair_hbm, mask_ref, smask_ref, we_ref, wog_ref, wop_ref, wa_ref, wb_ref, wo_ref,
     out_ref,
-    wet, wa_all, wb_all, wo_all, sent, got, wide, pair_t, normed_t, gates, back, owned, wide2,
+    pair_v, wa_all, wb_all, wo_all, sent_l, sent_r, got_l, got_r, wide_l, wide_r, pair_t, normed_t,
+    gates, back, owned, wide2,
     first_t, second_t, bias_rows, bias_send, bias_got, bias_t, query_t, keyed, value_t, attgate_t,
-    w_send, w_recv, a_send, a_recv, b_send, b_recv, c_send, c_recv, o_send, o_recv,
+    p_sem, w_send, w_recv, l_send, l_recv, r_send, r_recv, b_send, b_recv, c_send, c_recv,
+    o_send, o_recv,
 ):
     row = lax.axis_index("row")
     sub = lax.axis_index("sub")
     other = 1 - sub
-    count = 8
+    side = lax.div(row, 4)
+    place = lax.rem(row, 4)
     rows = 16
     half = 8
     step = rows // CHUNKS
 
-    def at_row(offset):
-        return lax.rem(row + offset, count)
-
-    def from_row(offset):
-        return lax.rem(row + count - offset, count)
-
-    barrier = pltpu.get_barrier_semaphore()
-    peers = [(o, d) for o in range(count) for d in range(2) if (o, d) != (0, 0)]
+    def p_copy(c):
+        part = pl.ds(c * step, step)
+        return pltpu.make_async_copy(pair_hbm.at[part], pair_v.at[part], p_sem.at[c])
+
+    for c in range(CHUNKS):
+        p_copy(c).start()
+
+    def place_to(dg):
+        return lax.rem(place + dg, 4)
+
+    def place_from(dg):
+        return lax.rem(place + 4 - dg, 4)
+
+    def side_of(ds):
+        return side if ds == 0 else 1 - side
+
+    def row_to(ds, dg):
+        return side_of(ds) * 4 + place_to(dg)
+
+    def row_from(ds, dg):
+        return side_of(ds) * 4 + place_from(dg)
 
     def peer_sub(d):
         return sub if d == 0 else other
 
-    for o, d in peers:
+    far = [(1, 3), (1, 2), (1, 1), (1, 0)]
+    near = [(0, 3), (0, 2), (0, 1)]
+    every = [(ds, dg, d) for ds, dg in far + near for d in (1, 0)] + [(0, 0, 1)]
+    around = [(dg, d) for dg in (3, 2, 1) for d in (1, 0)] + [(0, 1)]
+
+    barrier = pltpu.get_barrier_semaphore()
+    for ds, dg, d in every:
         pl.semaphore_signal(
-            barrier, inc=1, device_id={"row": at_row(o), "sub": peer_sub(d)}, device_id_type=MESH
-        )
-
-    turned_we = turned(we_ref[...])
-    gate_rows = [turned_we[128 * lr + 8 * p:128 * lr + 8 * p + 8] for p in range(8) for lr in range(2)]
-    value_rows = [
-        turned_we[128 * lr + 64 + 8 * p:128 * lr + 64 + 8 * p + 8] for p in range(8) for lr in range(2)
-    ]
-    wet[...] = jnp.concatenate(gate_rows + value_rows, axis=0).astype(jnp.bfloat16)
+            barrier, inc=1, device_id={"row": row_to(ds, dg), "sub": peer_sub(d)}, device_id_type=MESH
+        )
+
     mask_lanes = mask_ref[...].astype(jnp.float32)
-
-    def edge_row(i, carry):
-        x = pair_ref[i].T
+    edge_w = we_ref[...]
+
+    def edge_row(i):
+        x = pair_v[i].T
         pair_t[i] = x
         normed = norm_rows(x).astype(jnp.bfloat16)
         normed_t[i] = normed
-        projected = dot(wet[...], normed)
-        mask_row = smask_ref[row * rows + i].astype(jnp.float32)
-        edge = (mask_lanes * mask_row) * jax.nn.sigmoid(projected[:128]) * projected[128:]
-        edge = edge.astype(jnp.bfloat16)
-        for p in range(8):
-            sent[p, i] = edge[16 * p:16 * p + 16]
-        return carry
-
-    def a_copy(o, c, slot_from, slot_to):
+        projected = dot(edge_w, normed)
+        mask_row = mask_lanes * smask_ref[row * rows + i].astype(jnp.float32)
+        for q, sent in ((0, sent_l), (128, sent_r)):
+            edge = mask_row * jax.nn.sigmoid(projected[q:q + 64]) * projected[q + 64:q + 128]
+            edge = edge.astype(jnp.bfloat16)
+            for g in range(4):
+                sent[g, i] = edge[16 * g:16 * g + 16]
+
+    def r_copy(ds, dg, c, slot_from, slot_to):
         part = pl.ds(c * step, step)
         return pltpu.make_async_remote_copy(
-            src_ref=sent.at[slot_from, part],
-            dst_ref=got.at[slot_to, part],
-            send_sem=a_send.at[o, c],
-            recv_sem=a_recv.at[o, c],
-            device_id={"row": at_row(o)},
-            device_id_type=MESH,
-        )
-
-    def w_copy(k, src, dst):
-        return pltpu.make_async_remote_copy(
-            src_ref=src, dst_ref=dst, send_sem=w_send.at[k], recv_sem=w_recv.at[k],
+            src_ref=sent_r.at[slot_from, part], dst_ref=got_r.at[slot_to, part],
+            send_sem=r_send.at[ds * 4 + dg, c], recv_sem=r_recv.at[ds * 4 + dg, c],
+            device_id={"row": row_to(ds, dg)}, device_id_type=MESH,
+        )
+
+    def l_copy(dg, c, slot_from, slot_to):
+        part = pl.ds(c * step, step)
+        return pltpu.make_async_remote_copy(
+            src_ref=sent_l.at[slot_from, part], dst_ref=got_l.at[slot_to, part],
+            send_sem=l_send.at[dg, c], recv_sem=l_recv.at[dg, c],
+            device_id={"row": row_to(0, dg)}, device_id_type=MESH,
+        )
+
+    def w_copy(k, at):
+        src, dst = ((wa_ref, wa_all), (wb_ref, wb_all), (wo_ref, wo_all))[k]
+        return pltpu.make_async_remote_copy(
+            src_ref=src, dst_ref=dst.at[at], send_sem=w_send.at[k], recv_sem=w_recv.at[k],
             device_id={"sub": other}, device_id_type=MESH,
         )
 
-    order = [4, 3, 5, 2, 6, 1, 7]
     for c in range(CHUNKS):
-        lax.fori_loop(c * step, (c + 1) * step, edge_row, 0, unroll=2)
+        p_copy(c).wait()
+        for i in range(c * step, (c + 1) * step):
+            edge_row(i)
         if c == 0:
-            pl.semaphore_wait(barrier, len(peers))
-        for o in order:
-            a_copy(o, c, at_row(o), row).start()
-    for k, (src, dst) in enumerate(((wa_ref, wa_all), (wb_ref, wb_all), (wo_ref, wo_all))):
-        w_copy(k, src, dst.at[sub]).start()
+            pl.semaphore_wait(barrier, len(every))
+        for ds, dg in far + near:
+            r_copy(ds, dg, c, place_to(dg), row).start()
+            if ds == 0:
+                l_copy(dg, c, place_to(dg), place).start()
+    for k in range(3):
+        w_copy(k, sub).start()
 
     wa_all[sub] = wa_ref[...]
     wb_all[sub] = wb_ref[...]
     wo_all[sub] = wo_ref[...]
     outgate_t = turned(wog_ref[...]).astype(jnp.bfloat16)
-
-    def gate_row(i, carry):
+    for i in range(half):
         gates[i] = jax.nn.sigmoid(dot(outgate_t, normed_t[sub * half + i]))
-        return carry
-
-    lax.fori_loop(0, half, gate_row, 0, unroll=2)
     outproj_t = turned(wop_ref[...]).astype(jnp.bfloat16)
 
-    wide[pl.ds(pl.multiple_of(row * 256, 256), 256), :] = (
-        sent[row].reshape(256, 128).astype(jnp.float32)
-    )
-    for o in order[::-1]:
-        source = from_row(o)
+    def widen(dst, at, block):
+        dst[pl.ds(pl.multiple_of(at * 256, 256), 256), :] = (
+            block.reshape(256, 128).astype(jnp.float32)
+        )
+
+    widen(wide_l, place, sent_l[place])
+    widen(wide_r, row, sent_r[place])
+    for ds, dg in near[::-1] + far[::-1]:
+        source = row_from(ds, dg)
         for c in range(CHUNKS):
-            a_copy(o, c, source, source).wait_recv()
-        wide[pl.ds(pl.multiple_of(source * 256, 256), 256), :] = (
-            got[source].reshape(256, 128).astype(jnp.float32)
-        )
-
-    for pair_of in range(4):
+            r_copy(ds, dg, c, place_to(dg), source).wait_recv()
+        widen(wide_r, source, got_r[source])
+        if ds == 0:
+            for c in range(CHUNKS):
+                l_copy(dg, c, place_to(dg), place_from(dg)).wait_recv()
+            widen(wide_l, place_from(dg), got_l[place_from(dg)])
+
+    for pair_of in range(8):
         sums = []
         for h in (2 * pair_of, 2 * pair_of + 1):
-            left = wide[pl.ds(h, 128, stride=16), :].astype(jnp.bfloat16)
-            right = wide[pl.ds(8 + h, 128, stride=16), :].astype(jnp.bfloat16)
+            left = wide_l[pl.ds(h, 64, stride=16), :].astype(jnp.bfloat16)
+            right = wide_r[pl.ds(h, 128, stride=16), :].astype(jnp.bfloat16)
             total = lax.dot_general(
                 left, right, (((1,), (1,)), ((), ())), preferred_element_type=jnp.float32
             )
-            sums.append(total.reshape(16, 8, 128))
+            sums.append(total.reshape(8, 8, 128))
         back[:, pl.ds(16 * pair_of, 16), :] = jnp.concatenate(sums, axis=1).astype(jnp.bfloat16)
 
-    def b_copy(k, o, d, src, dst):
+    def b_copy(k, dg, d, src, dst):
         return pltpu.make_async_remote_copy(
             src_ref=back.at[src], dst_ref=owned.at[dst], send_sem=b_send.at[k], recv_sem=b_recv.at[k],
-            device_id={"row": at_row(o), "sub": peer_sub(d)}, device_id_type=MESH,
-        )
-
-    ranked = [(o, d) for o in order for d in (1, 0)] + [(0, 1)]
-    for k, (o, d) in enumerate(ranked):
-        b_copy(k, o, d, at_row(o) * 2 + peer_sub(d), sub * 8 + row).start()
-    wide2[pl.ds(pl.multiple_of((sub * 8 + row) * 64, 64), 64), :] = (
-        back[row * 2 + sub].astype(jnp.float32)
-    )
-
-    for k, (src, dst) in enumerate(((wa_ref, wa_all), (wb_ref, wb_all), (wo_ref, wo_all))):
-        w_copy(k, src, dst.at[other]).wait_recv()
-    wat = [turned(wa_all[s]).astype(jnp.bfloat16) for s in range(2)]
+            device_id={"row": row_to(0, dg), "sub": peer_sub(d)}, device_id_type=MESH,
+        )
+
+    def widen2(at, block):
+        wide2[pl.ds(pl.multiple_of(at * 128, 128), 128), :] = block.astype(jnp.float32)
+
+    for k, (dg, d) in enumerate(around):
+        b_copy(k, dg, d, place_to(dg) * 2 + peer_sub(d), sub * 4 + place).start()
+    widen2(sub * 4 + place, back[place * 2 + sub])
+
+    for k in range(3):
+        w_copy(k, other).wait_recv()
     attend_t = jnp.concatenate(
-        [wat[s][64 * q:64 * q + 64] for q in range(4) for s in range(2)], axis=0
+        [wa_all[s, 64 * q:64 * q + 64] for q in range(4) for s in range(2)], axis=0
     )
     bias_w = wb_all[...].reshape(32, 128)
     attout_t = turned(wo_all[...].reshape(128, 128)).astype(jnp.bfloat16)
 
-    for k in reversed(range(len(ranked))):
-        o, d = ranked[k]
-        source = peer_sub(d) * 8 + from_row(o)
-        b_copy(k, o, d, 0, source).wait_recv()
-        wide2[pl.ds(pl.multiple_of(source * 64, 64), 64), :] = owned[source].astype(jnp.float32)
+    for k in reversed(range(len(around))):
+        dg, d = around[k]
+        source = peer_sub(d) * 4 + place_from(dg)
+        b_copy(k, dg, d, 0, source).wait_recv()
+        widen2(source, owned[source])
 
     for i in range(half):
         edgenorm = norm_rows(wide2[pl.ds(i, 128, stride=8), :]).astype(jnp.bfloat16)
@@ -179,30 +206,28 @@
             bias_rows[n * 8 + i:n * 8 + i + 1, :] = bias[r:r + 1]
     bias_send[...] = bias_rows[...].astype(jnp.bfloat16)
 
-    def c_copy(k, o, d, dst):
-        return pltpu.make_async_remote_copy(
-            src_ref=bias_send, dst_ref=bias_got.at[dst], send_sem=c_send.at[k], recv_sem=c_recv.at[k],
-            device_id={"row": at_row(o), "sub": peer_sub(d)}, device_id_type=MESH,
-        )
-
-    for k, (o, d) in enumerate(ranked):
-        c_copy(k, o, d, row * 2 + sub).start()
-
-    def project_row(i, carry):
+    def c_copy(k, at):
+        ds, dg, d = every[k]
+        return pltpu.make_async_remote_copy(
+            src_ref=bias_send, dst_ref=bias_got.at[at], send_sem=c_send.at[k], recv_sem=c_recv.at[k],
+            device_id={"row": row_to(ds, dg), "sub": peer_sub(d)}, device_id_type=MESH,
+        )
+
+    mine = row * 2 + sub
+    for k in range(len(every)):
+        c_copy(k, mine).start()
+    bias_got[mine] = bias_send[...]
+
+    for i in range(half):
         projected = dot(attend_t, second_t[i])
         query_t[i] = projected[:128].astype(jnp.bfloat16)
         keyed[i] = projected[128:256].T.astype(jnp.bfloat16)
         value_t[i] = projected[256:384].astype(jnp.bfloat16)
         attgate_t[i] = jax.nn.sigmoid(projected[384:])
-        return carry
-
-    lax.fori_loop(0, half, project_row, 0, unroll=2)
-
-    mine = row * 2 + sub
-    bias_got[mine] = bias_send[...]
-    for k in reversed(range(len(ranked))):
-        o, d = ranked[k]
-        c_copy(k, o, d, from_row(o) * 2 + peer_sub(d)).wait_recv()
+
+    for k in reversed(range(len(every))):
+        ds, dg, d = every[k]
+        c_copy(k, row_from(ds, dg) * 2 + peer_sub(d)).wait_recv()
     maskbias = 1000000000.0 * (mask_lanes - 1.0)
     all_bias = bias_got[...].astype(jnp.float32)
     for n in range(4):
@@ -217,11 +242,12 @@
             device_id={"sub": other}, device_id_type=MESH,
         )
 
-    def attend_row(i, carry):
+    nothing = jnp.zeros((32, 128), jnp.bfloat16)
+
+    def attend_row(i):
         query = query_t[i]
         key = keyed[i]
         value = value_t[i]
-        nothing = jnp.zeros((32, 128), jnp.bfloat16)
         mixed = []
         for n in range(4):
             head = jnp.concatenate(
@@ -234,19 +260,24 @@
             mixed.append(dot(value[32 * n:32 * n + 32], weights.astype(jnp.bfloat16)) / total)
         mixed = (jnp.concatenate(mixed, axis=0) * attgate_t[i]).astype(jnp.bfloat16)
         out_ref[sub * half + i] = (first_t[i] + dot(attout_t, mixed)).T
-        o_copy(i, sub).start()
-        return carry
-
-    lax.fori_loop(0, half, attend_row, 0, unroll=2)
-
-    for k, (src, dst) in enumerate(((wa_ref, wa_all), (wb_ref, wb_all), (wo_ref, wo_all))):
-        w_copy(k, src, dst.at[sub]).wait_send()
+
+    for i in range(half):
+        attend_row(i)
+        if i % 2 == 1:
+            o_copy(i - 1, sub).start()
+            o_copy(i, sub).start()
+
+    for k in range(3):
+        w_copy(k, sub).wait_send()
     for c in range(CHUNKS):
-        for o in order:
-            a_copy(o, c, at_row(o), row).wait_send()
-    for k, (o, d) in enumerate(ranked):
-        b_copy(k, o, d, at_row(o) * 2 + peer_sub(d), sub * 8 + row).wait_send()
-        c_copy(k, o, d, row * 2 + sub).wait_send()
+        for ds, dg in far + near:
+            r_copy(ds, dg, c, place_to(dg), row).wait_send()
+            if ds == 0:
+                l_copy(dg, c, place_to(dg), place).wait_send()
+    for k, (dg, d) in enumerate(around):
+        b_copy(k, dg, d, place_to(dg) * 2 + peer_sub(d), sub * 4 + place).wait_send()
+    for k in range(len(every)):
+        c_copy(k, mine).wait_send()
     for i in range(half):
         o_copy(i, sub).wait_send()
         o_copy(i, other).wait_recv()
@@ -260,21 +291,25 @@
     return pl.pallas_call(
         fused_kernel,
         out_shape=jax.ShapeDtypeStruct(pair.shape, f32),
-        in_specs=[vmem, vmem, pl.BlockSpec(memory_space=pltpu.SMEM)] + [vmem] * 6,
+        in_specs=[pl.BlockSpec(memory_space=pltpu.HBM), vmem, pl.BlockSpec(memory_space=pltpu.SMEM)]
+        + [vmem] * 6,
         out_specs=vmem,
         scratch_shapes=[
-            pltpu.VMEM((256, 128), bf16),
-            pltpu.VMEM((2, 128, 256), bf16),
+            pltpu.VMEM((16, 128, 128), f32),
+            pltpu.VMEM((2, 256, 128), bf16),
             pltpu.VMEM((2, 16, 128), bf16),
             pltpu.VMEM((2, 64, 128), bf16),
+            pltpu.VMEM((4, 16, 16, 128), bf16),
+            pltpu.VMEM((4, 16, 16, 128), bf16),
+            pltpu.VMEM((4, 16, 16, 128), bf16),
             pltpu.VMEM((8, 16, 16, 128), bf16),
-            pltpu.VMEM((8, 16, 16, 128), bf16),
+            pltpu.VMEM((1024, 128), f32),
             pltpu.VMEM((2048, 128), f32),
             pltpu.VMEM((16, 128, 128), f32),
             pltpu.VMEM((16, 128, 128), bf16),
             pltpu.VMEM((8, 128, 128), f32),
-            pltpu.VMEM((16, 64, 128), bf16),
-            pltpu.VMEM((16, 64, 128), bf16),
+            pltpu.VMEM((8, 128, 128), bf16),
+            pltpu.VMEM((8, 128, 128), bf16),
             pltpu.VMEM((1024, 128), f32),
             pltpu.VMEM((8, 128, 128), f32),
             pltpu.VMEM((8, 128, 128), bf16),
@@ -286,9 +321,11 @@
             pltpu.VMEM((8, 128, 128), bf16),
             pltpu.VMEM((8, 128, 128), bf16),
             pltpu.VMEM((8, 128, 128), f32),
+            dma((CHUNKS,)),
             dma((3,)), dma((3,)),
+            dma((4, CHUNKS)), dma((4, CHUNKS)),
             dma((8, CHUNKS)), dma((8, CHUNKS)),
-            dma((15,)), dma((15,)),
+            dma((7,)), dma((7,)),
             dma((15,)), dma((15,)),
             dma((8,)), dma((8,)),
         ],
@@ -297,8 +334,8 @@
         ),
         name="window",
     )(
-        pair, mask.reshape(1, 128), mask, w_edges.reshape(128, 256), w_outgate, w_outproj,
-        w_attend.reshape(128, 256), bias_rows, w_attout,
+        pair, mask.reshape(1, 128), mask, w_edges.transpose(1, 2, 0).reshape(256, 128), w_outgate,
+        w_outproj, w_attend.transpose(1, 2, 0).reshape(256, 128), bias_rows, w_attout,
     )
 
 

time: 45.1 us -> 43.9 us (0.973)
  Pallas kernels: 40.1 us -> 36 us
  local copies, waits for them, and re-layouts: 4.57 us -> 7.42 us
    pallas_call x1, Pallas kernels: 40.1 us -> 36 us  [fused_body(): pl.pallas_call(fused_kernel, out_shape=jax.ShapeDtypeStruct(pair.shape, f...]
    unnamed x15 -> x17, local copies, waits for them, and re-layouts: 3.49 us -> 7.41 us
    reshape x2 -> x0, local copies, waits for them, and re-layouts: 1.07 us -> none  [the longest x1 0.97 us: fused_body(): w_edges.reshape(128, 256)]
where the time goes in v2:
time: 43.9 us; the launch traced here: 43.4 us
  Pallas kernels  36 us (82%)
  local copies, waits for them, and re-layouts  7.42 us (17%)
    pallas_call x1, Pallas kernels, fused_body(): pl.pallas_call(fused_kernel, out_shape=jax.ShapeDtypeStruct(pair.shape, f...  36 us
    unnamed x17, local copies, waits for them, and re-layouts  7.41 us

profile of v2, /device:TPU:0, one launch (start us, length us, event | category | flops | bytes accessed | tf_op | source)
XLA Modules:
  0.0 43.4 jit_solution(6289787931024131381)
XLA Ops:
  0.0 0.0 copy-start.7
  0.0 0.7 %copy-done.7 = bf16[128,2]{0,1:T(2,128)(2,1)S(1)} copy-done((bf16[128,2]{0,1:T(2,128)(2,1)S(1)}, bf16[128,2]{0,1:T(2,128)(2,1)}, u32[]{:S(2)}) %copy-start.7) | copy-done | bytes 536
  0.7 0.0 copy-start.6
  0.7 0.6 %copy-done.6 = s32[128]{0:T(128)S(1)} copy-done((s32[128]{0:T(128)S(1)}, s32[128]{0:T(128)}, u32[]{:S(2)}) %copy-start.6) | copy-done | bytes 536
  1.3 0.0 copy-start
  1.3 1.2 %copy-done = f32[16,128,128]{2,1,0:T(8,128)S(1)} copy-done((f32[16,128,128]{2,1,0:T(8,128)S(1)}, f32[16,128,128]{2,1,0:T(8,128)}, u32[]{:S(2)}) %copy-start) | copy-done | bytes 1048600
  2.5 0.0 copy-start.1
  2.5 0.8 %copy-done.1 = bf16[128,4,64]{0,2,1:T(8,128)(2,1)S(1)} copy-done((bf16[128,4,64]{0,2,1:T(8,128)(2,1)S(1)}, bf16[128,4,64]{0,2,1:T(8,128)(2,1)}, u32[]{:S(2)}) %copy-start.1) | copy-done | bytes 65560
  3.4 0.0 copy-start.2
  3.4 0.8 %copy-done.2 = bf16[128,4,64]{0,2,1:T(8,128)(2,1)S(1)} copy-done((bf16[128,4,64]{0,2,1:T(8,128)(2,1)S(1)}, bf16[128,4,64]{0,2,1:T(8,128)(2,1)}, u32[]{:S(2)}) %copy-start.2) | copy-done | bytes 65560
  4.2 0.0 copy-start.3
  4.2 0.8 %copy-done.3 = bf16[128,128]{1,0:T(8,128)(2,1)S(1)} copy-done((bf16[128,128]{1,0:T(8,128)(2,1)S(1)}, bf16[128,128]{1,0:T(8,128)(2,1)}, u32[]{:S(2)}) %copy-start.3) | copy-done | bytes 32792
  5.0 0.0 copy-start.4
  5.0 0.8 %copy-done.4 = bf16[128,128]{1,0:T(8,128)(2,1)S(1)} copy-done((bf16[128,128]{1,0:T(8,128)(2,1)S(1)}, bf16[128,128]{1,0:T(8,128)(2,1)}, u32[]{:S(2)}) %copy-start.4) | copy-done | bytes 32792
  5.7 0.0 copy-start.5
  5.7 0.7 %copy-done.5 = bf16[64,128]{1,0:T(8,128)(2,1)S(1)} copy-done((bf16[64,128]{1,0:T(8,128)(2,1)S(1)}, bf16[64,128]{1,0:T(8,128)(2,1)}, u32[]{:S(2)}) %copy-start.5) | copy-done | bytes 16408
  6.5 36.0 %window.1 = f32[16,128,128]{2,1,0:T(8,128)S(1)} custom-call(f32[16,128,128]{2,1,0:T(8,128)S(1)} %copy-done, s32[1,128]{1,0:T(1,128)S(1)} %bitcast.10, s32[128]{0:T(128)S(1)} %copy-done.6, bf16[256,128]{1,0:T(8,128)(2,1)S(1)} %bitcast.8, bf16[128,128]{1,0:T(8,128)(2,1)S(1)} %copy-done.3, bf16[128,128]{1,0:T(8,128)(2,1)S(1)} %copy-done.4, ...), custom_call_target="tpu_custom_call" | custom-call | tf_op jit(solution)/shard_map/window/pallas_call | solution.py:291
  42.4 1.0 %copy.10 = f32[16,128,128]{2,1,0:T(8,128)} copy(f32[16,128,128]{2,1,0:T(8,128)S(1)} %window.1) | data formatting | bytes 2097152
  (1 shorter events, 0.0 us)
Async XLA Ops:
  0.0 0.7 %copy-start.7 = (bf16[128,2]{0,1:T(2,128)(2,1)S(1)}, bf16[128,2]{0,1:T(2,128)(2,1)}, u32[]{:S(2)}) copy-start(bf16[128,2]{0,1:T(2,128)(2,1)} %param.14) | copy-start | bytes 1540
  0.7 0.7 %copy-start.6 = (s32[128]{0:T(128)S(1)}, s32[128]{0:T(128)}, u32[]{:S(2)}) copy-start(s32[128]{0:T(128)} %smask_ref.1) | copy-start | bytes 1540
  1.3 1.2 %copy-start = (f32[16,128,128]{2,1,0:T(8,128)S(1)}, f32[16,128,128]{2,1,0:T(8,128)}, u32[]{:S(2)}) copy-start(f32[16,128,128]{2,1,0:T(8,128)} %pair_hbm.1) | copy-start | bytes 3145732
  2.5 0.8 %copy-start.1 = (bf16[128,4,64]{0,2,1:T(8,128)(2,1)S(1)}, bf16[128,4,64]{0,2,1:T(8,128)(2,1)}, u32[]{:S(2)}) copy-start(bf16[128,4,64]{0,2,1:T(8,128)(2,1)} %param.10) | copy-start | bytes 196612
  3.4 0.8 %copy-start.2 = (bf16[128,4,64]{0,2,1:T(8,128)(2,1)S(1)}, bf16[128,4,64]{0,2,1:T(8,128)(2,1)}, u32[]{:S(2)}) copy-start(bf16[128,4,64]{0,2,1:T(8,128)(2,1)} %param.13) | copy-start | bytes 196612
  4.2 0.8 %copy-start.3 = (bf16[128,128]{1,0:T(8,128)(2,1)S(1)}, bf16[128,128]{1,0:T(8,128)(2,1)}, u32[]{:S(2)}) copy-start(bf16[128,128]{1,0:T(8,128)(2,1)} %wog_ref.1) | copy-start | bytes 98308
  5.0 0.8 %copy-start.4 = (bf16[128,128]{1,0:T(8,128)(2,1)S(1)}, bf16[128,128]{1,0:T(8,128)(2,1)}, u32[]{:S(2)}) copy-start(bf16[128,128]{1,0:T(8,128)(2,1)} %wop_ref.1) | copy-start | bytes 98308
  5.7 0.7 %copy-start.5 = (bf16[64,128]{1,0:T(8,128)(2,1)S(1)}, bf16[64,128]{1,0:T(8,128)(2,1)}, u32[]{:S(2)}) copy-start(bf16[64,128]{1,0:T(8,128)(2,1)} %wo_ref.1) | copy-start | bytes 49156

commit v3 on v2

--- a/solution.py
+++ b/solution.py
@@ -7,7 +7,8 @@
 
 EPS = 1e-05
 MESH = pl.DeviceIdType.MESH
-CHUNKS = 4
+CHUNKS = 1
+LOADS = 4
 
 
 def dot(a, b):
@@ -26,12 +27,13 @@
 
 
 def fused_kernel(
-    pair_hbm, mask_ref, smask_ref, we_ref, wog_ref, wop_ref, wa_ref, wb_ref, wo_ref,
+    pair_hbm, mask_hbm, we_hbm, wog_hbm, wop_hbm, wa_hbm, wb_hbm, wo_hbm,
     out_ref,
+    mask_ref, we_ref, wog_ref, wop_ref, wa_ref, wb_in, wb_ref, wo_ref, scores_t,
     pair_v, wa_all, wb_all, wo_all, sent_l, sent_r, got_l, got_r, wide_l, wide_r, pair_t, normed_t,
     gates, back, owned, wide2,
     first_t, second_t, bias_rows, bias_send, bias_got, bias_t, query_t, keyed, value_t, attgate_t,
-    p_sem, w_send, w_recv, l_send, l_recv, r_send, r_recv, b_send, b_recv, c_send, c_recv,
+    i_sem, p_sem, w_send, w_recv, l_send, l_recv, r_send, r_recv, b_send, b_recv, c_send, c_recv,
     o_send, o_recv,
 ):
     row = lax.axis_index("row")
@@ -43,12 +45,26 @@
     half = 8
     step = rows // CHUNKS
 
+    load = rows // LOADS
+
     def p_copy(c):
-        part = pl.ds(c * step, step)
+        part = pl.ds(c * load, load)
         return pltpu.make_async_copy(pair_hbm.at[part], pair_v.at[part], p_sem.at[c])
 
-    for c in range(CHUNKS):
+    def i_copy(k):
+        src, dst = (
+            (we_hbm, we_ref), (mask_hbm, mask_ref), (wog_hbm, wog_ref), (wop_hbm, wop_ref),
+            (wa_hbm, wa_ref), (wb_hbm, wb_in), (wo_hbm, wo_ref),
+        )[k]
+        return pltpu.make_async_copy(src, dst, i_sem.at[k])
+
+    p_copy(0).start()
+    i_copy(0).start()
+    i_copy(1).start()
+    for c in range(1, LOADS):
         p_copy(c).start()
+    for k in range(2, 7):
+        i_copy(k).start()
 
     def place_to(dg):
         return lax.rem(place + dg, 4)
@@ -74,12 +90,19 @@
     around = [(dg, d) for dg in (3, 2, 1) for d in (1, 0)] + [(0, 1)]
 
     barrier = pltpu.get_barrier_semaphore()
-    for ds, dg, d in every:
+    greeted = [(ds, dg, 0) for ds, dg in far + near] + [(0, 0, 1)]
+    for ds, dg, d in greeted:
         pl.semaphore_signal(
             barrier, inc=1, device_id={"row": row_to(ds, dg), "sub": peer_sub(d)}, device_id_type=MESH
         )
 
+    i_copy(0).wait()
+    i_copy(1).wait()
     mask_lanes = mask_ref[...].astype(jnp.float32)
+    here = lax.broadcasted_iota(jnp.int32, (rows, 128), 1) == (
+        row * rows + lax.broadcasted_iota(jnp.int32, (rows, 128), 0)
+    )
+    mask_rows = jnp.sum(jnp.where(here, mask_lanes, 0.0), axis=1, keepdims=True)
     edge_w = we_ref[...]
 
     def edge_row(i):
@@ -88,7 +111,7 @@
         normed = norm_rows(x).astype(jnp.bfloat16)
         normed_t[i] = normed
         projected = dot(edge_w, normed)
-        mask_row = mask_lanes * smask_ref[row * rows + i].astype(jnp.float32)
+        mask_row = mask_lanes * mask_rows[i:i + 1]
         for q, sent in ((0, sent_l), (128, sent_r)):
             edge = mask_row * jax.nn.sigmoid(projected[q:q + 64]) * projected[q + 64:q + 128]
             edge = edge.astype(jnp.bfloat16)
@@ -118,16 +141,21 @@
             device_id={"sub": other}, device_id_type=MESH,
         )
 
+    for c in range(LOADS):
+        p_copy(c).wait()
+        for i in range(c * load, (c + 1) * load):
+            edge_row(i)
+    pl.semaphore_wait(barrier, len(greeted))
     for c in range(CHUNKS):
-        p_copy(c).wait()
-        for i in range(c * step, (c + 1) * step):
-            edge_row(i)
-        if c == 0:
-            pl.semaphore_wait(barrier, len(every))
         for ds, dg in far + near:
             r_copy(ds, dg, c, place_to(dg), row).start()
             if ds == 0:
                 l_copy(dg, c, place_to(dg), place).start()
+    for k in range(2, 7):
+        i_copy(k).wait()
+    wb_ref[...] = jnp.concatenate(
+        [wb_in[...].astype(jnp.float32), jnp.zeros((14, 128), jnp.float32)], axis=0
+    ).astype(jnp.bfloat16)
     for k in range(3):
         w_copy(k, sub).start()
 
@@ -213,6 +241,7 @@
             device_id={"row": row_to(ds, dg), "sub": peer_sub(d)}, device_id_type=MESH,
         )
 
+    scale = 1.0 / (32.0 ** 0.5)
     mine = row * 2 + sub
     for k in range(len(every)):
         c_copy(k, mine).start()
@@ -224,6 +253,15 @@
         keyed[i] = projected[128:256].T.astype(jnp.bfloat16)
         value_t[i] = projected[256:384].astype(jnp.bfloat16)
         attgate_t[i] = jax.nn.sigmoid(projected[384:])
+    nothing = jnp.zeros((32, 128), jnp.bfloat16)
+    for i in range(half):
+        query = query_t[i]
+        key = keyed[i]
+        for n in range(4):
+            head = jnp.concatenate(
+                [query[32 * m:32 * m + 32] if m == n else nothing for m in range(4)], axis=0
+            )
+            scores_t[i, n] = dot(key, head) * scale
 
     for k in reversed(range(len(every))):
         ds, dg, d = every[k]
@@ -233,8 +271,6 @@
     for n in range(4):
         bias_t[n] = (all_bias[:, n * 8:n * 8 + 8, :].reshape(128, 128) + maskbias).T
 
-    scale = 1.0 / (32.0 ** 0.5)
-
     def o_copy(i, at):
         return pltpu.make_async_remote_copy(
             src_ref=out_ref.at[at * half + i], dst_ref=out_ref.at[at * half + i],
@@ -242,18 +278,11 @@
             device_id={"sub": other}, device_id_type=MESH,
         )
 
-    nothing = jnp.zeros((32, 128), jnp.bfloat16)
-
     def attend_row(i):
-        query = query_t[i]
-        key = keyed[i]
         value = value_t[i]
         mixed = []
         for n in range(4):
-            head = jnp.concatenate(
-                [query[32 * m:32 * m + 32] if m == n else nothing for m in range(4)], axis=0
-            )
-            scores = dot(key, head) * scale + bias_t[n]
+            scores = scores_t[i, n] + bias_t[n]
             top = jnp.max(scores, axis=0, keepdims=True)
             weights = jnp.exp(scores - top)
             total = jnp.sum(weights, axis=0, keepdims=True)
@@ -286,15 +315,22 @@
 def fused_body(pair, mask, w_edges, w_outgate, w_outproj, w_attend, w_bias, w_attout):
     f32, bf16 = jnp.float32, jnp.bfloat16
     vmem = pl.BlockSpec(memory_space=pltpu.VMEM)
-    bias_rows = jnp.pad(w_bias.T, ((0, 14), (0, 0)))
     dma = pltpu.SemaphoreType.DMA
     return pl.pallas_call(
         fused_kernel,
         out_shape=jax.ShapeDtypeStruct(pair.shape, f32),
-        in_specs=[pl.BlockSpec(memory_space=pltpu.HBM), vmem, pl.BlockSpec(memory_space=pltpu.SMEM)]
-        + [vmem] * 6,
+        in_specs=[pl.BlockSpec(memory_space=pltpu.HBM)] * 8,
         out_specs=vmem,
         scratch_shapes=[
+            pltpu.VMEM((1, 128), jnp.int32),
+            pltpu.VMEM((256, 128), bf16),
+            pltpu.VMEM((128, 128), bf16),
+            pltpu.VMEM((128, 128), bf16),
+            pltpu.VMEM((256, 128), bf16),
+            pltpu.VMEM((2, 128), bf16),
+            pltpu.VMEM((16, 128), bf16),
+            pltpu.VMEM((64, 128), bf16),
+            pltpu.VMEM((8, 4, 128, 128), f32),
             pltpu.VMEM((16, 128, 128), f32),
             pltpu.VMEM((2, 256, 128), bf16),
             pltpu.VMEM((2, 16, 128), bf16),
@@ -321,7 +357,8 @@
             pltpu.VMEM((8, 128, 128), bf16),
             pltpu.VMEM((8, 128, 128), bf16),
             pltpu.VMEM((8, 128, 128), f32),
-            dma((CHUNKS,)),
+            dma((7,)),
+            dma((LOADS,)),
             dma((3,)), dma((3,)),
             dma((4, CHUNKS)), dma((4, CHUNKS)),
             dma((8, CHUNKS)), dma((8, CHUNKS)),
@@ -330,12 +367,12 @@
             dma((8,)), dma((8,)),
         ],
         compiler_params=pltpu.CompilerParams(
-            collective_id=0, has_side_effects=True, vmem_limit_bytes=40 * 1024 * 1024
+            collective_id=0, has_side_effects=True, vmem_limit_bytes=60 * 1024 * 1024
         ),
         name="window",
     )(
-        pair, mask.reshape(1, 128), mask, w_edges.transpose(1, 2, 0).reshape(256, 128), w_outgate,
-        w_outproj, w_attend.transpose(1, 2, 0).reshape(256, 128), bias_rows, w_attout,
+        pair, mask.reshape(1, 128), w_edges.transpose(1, 2, 0).reshape(256, 128), w_outgate,
+        w_outproj, w_attend.transpose(1, 2, 0).reshape(256, 128), w_bias.T, w_attout,
     )
 
 

time: 43.9 us -> 36.9 us (0.84)
  local copies, waits for them, and re-layouts: 7.42 us -> 2.3 us
  Pallas kernels: 36 us -> 34.5 us
    unnamed x17 -> x1, local copies, waits for them, and re-layouts: 7.41 us -> 2.3 us
    pallas_call x1, Pallas kernels: 36 us -> 34.5 us  [fused_body(): pl.pallas_call(fused_kernel, out_shape=jax.ShapeDtypeStruct(pair.shape, f...]
where the time goes in v3:
time: 36.9 us; the launch traced here: 36.8 us
  Pallas kernels  34.5 us (93%)
  local copies, waits for them, and re-layouts  2.3 us (6%)
    pallas_call x1, Pallas kernels, fused_body(): pl.pallas_call(fused_kernel, out_shape=jax.ShapeDtypeStruct(pair.shape, f...  34.5 us
    unnamed x1, local copies, waits for them, and re-layouts  2.3 us

profile of v3, /device:TPU:0, one launch (start us, length us, event | category | flops | bytes accessed | tf_op | source)
XLA Modules:
  0.0 36.8 jit_solution(5454090781021402930)
XLA Ops:
  0.0 34.5 %window.1 = f32[16,128,128]{2,1,0:T(8,128)} custom-call(f32[16,128,128]{2,1,0:T(8,128)} %pair_hbm.1, s32[1,128]{1,0:T(1,128)} %bitcast.10, bf16[256,128]{1,0:T(8,128)(2,1)} %bitcast.8, bf16[128,128]{1,0:T(8,128)(2,1)} %wog_hbm.1, bf16[128,128]{1,0:T(8,128)(2,1)} %wop_hbm.1, bf16[256,128]{1,0:T(8,128)(2,1)} %bitcast.9, bf16[2,128]{1,0:T(2,128)(2,1)} %bitcast.11, ...), custom_call_target="tpu_custom_call" | custom-call | tf_op jit(solution)/shard_map/window/pallas_call | solution.py:319
  34.5 2.3 %copy.10 = f32[16,128,128]{2,1,0:T(8,128)} copy(f32[16,128,128]{2,1,0:T(8,128)} %window.1) | data formatting | bytes 2097152

commit v4 on v3

--- a/solution.py
+++ b/solution.py
@@ -32,9 +32,9 @@
     mask_ref, we_ref, wog_ref, wop_ref, wa_ref, wb_in, wb_ref, wo_ref, scores_t,
     pair_v, wa_all, wb_all, wo_all, sent_l, sent_r, got_l, got_r, wide_l, wide_r, pair_t, normed_t,
     gates, back, owned, wide2,
-    first_t, second_t, bias_rows, bias_send, bias_got, bias_t, query_t, keyed, value_t, attgate_t,
+    change_t, second_t, bias_rows, bias_send, bias_got, bias_t, query_t, keyed, value_t, attgate_t,
     i_sem, p_sem, w_send, w_recv, l_send, l_recv, r_send, r_recv, b_send, b_recv, c_send, c_recv,
-    o_send, o_recv,
+    o_send, o_recv, own_sem, out_v,
 ):
     row = lax.axis_index("row")
     sub = lax.axis_index("sub")
@@ -224,8 +224,9 @@
 
     for i in range(half):
         edgenorm = norm_rows(wide2[pl.ds(i, 128, stride=8), :]).astype(jnp.bfloat16)
-        first = pair_t[sub * half + i] + gates[i] * dot(outproj_t, edgenorm)
-        first_t[i] = first
+        change = gates[i] * dot(outproj_t, edgenorm)
+        change_t[i] = change
+        first = pair_t[sub * half + i] + change
         second = norm_rows(first).astype(jnp.bfloat16)
         second_t[i] = second
         bias = dot(bias_w, second)
@@ -273,10 +274,13 @@
 
     def o_copy(i, at):
         return pltpu.make_async_remote_copy(
-            src_ref=out_ref.at[at * half + i], dst_ref=out_ref.at[at * half + i],
+            src_ref=out_v.at[i], dst_ref=out_ref.at[at * half + i],
             send_sem=o_send.at[i], recv_sem=o_recv.at[i],
             device_id={"sub": other}, device_id_type=MESH,
         )
+
+    def own_copy(i):
+        return pltpu.make_async_copy(out_v.at[i], out_ref.at[sub * half + i], own_sem.at[i])
 
     def attend_row(i):
         value = value_t[i]
@@ -288,13 +292,15 @@
             total = jnp.sum(weights, axis=0, keepdims=True)
             mixed.append(dot(value[32 * n:32 * n + 32], weights.astype(jnp.bfloat16)) / total)
         mixed = (jnp.concatenate(mixed, axis=0) * attgate_t[i]).astype(jnp.bfloat16)
-        out_ref[sub * half + i] = (first_t[i] + dot(attout_t, mixed)).T
+        out_v[i] = (change_t[i] + dot(attout_t, mixed)).T
 
     for i in range(half):
         attend_row(i)
         if i % 2 == 1:
             o_copy(i - 1, sub).start()
             o_copy(i, sub).start()
+            own_copy(i - 1).start()
+            own_copy(i).start()
 
     for k in range(3):
         w_copy(k, sub).wait_send()
@@ -308,19 +314,19 @@
     for k in range(len(every)):
         c_copy(k, mine).wait_send()
     for i in range(half):
+        own_copy(i).wait()
         o_copy(i, sub).wait_send()
         o_copy(i, other).wait_recv()
 
 
 def fused_body(pair, mask, w_edges, w_outgate, w_outproj, w_attend, w_bias, w_attout):
     f32, bf16 = jnp.float32, jnp.bfloat16
-    vmem = pl.BlockSpec(memory_space=pltpu.VMEM)
     dma = pltpu.SemaphoreType.DMA
-    return pl.pallas_call(
+    change = pl.pallas_call(
         fused_kernel,
         out_shape=jax.ShapeDtypeStruct(pair.shape, f32),
         in_specs=[pl.BlockSpec(memory_space=pltpu.HBM)] * 8,
-        out_specs=vmem,
+        out_specs=pl.BlockSpec(memory_space=pltpu.HBM),
         scratch_shapes=[
             pltpu.VMEM((1, 128), jnp.int32),
             pltpu.VMEM((256, 128), bf16),
@@ -364,7 +370,8 @@
             dma((8, CHUNKS)), dma((8, CHUNKS)),
             dma((7,)), dma((7,)),
             dma((15,)), dma((15,)),
-            dma((8,)), dma((8,)),
+            dma((8,)), dma((8,)), dma((8,)),
+            pltpu.VMEM((8, 128, 128), f32),
         ],
         compiler_params=pltpu.CompilerParams(
             collective_id=0, has_side_effects=True, vmem_limit_bytes=60 * 1024 * 1024
@@ -374,6 +381,7 @@
         pair, mask.reshape(1, 128), w_edges.transpose(1, 2, 0).reshape(256, 128), w_outgate,
         w_outproj, w_attend.transpose(1, 2, 0).reshape(256, 128), w_bias.T, w_attout,
     )
+    return pair + change
 
 
 def fits(mesh):

time: 36.9 us -> 36.2 us (0.981)
  other arithmetic: 0 us -> 2.33 us
  local copies, waits for them, and re-layouts: 2.3 us -> 0.01 us
  Pallas kernels: 34.5 us -> 33.7 us
    add x0 -> x1, other arithmetic: none -> 2.33 us  [fused_body(): return pair + change]
    unnamed x1 -> x2, local copies, waits for them, and re-layouts: 2.3 us -> 0.01 us
    pallas_call x1, Pallas kernels: 34.5 us -> 33.7 us  [fused_body(): pl.pallas_call(fused_kernel, out_shape=jax.ShapeDtypeStruct(pair.shape, f...]
where the time goes in v4:
time: 36.2 us; the launch traced here: 36.1 us
  Pallas kernels  33.7 us (93%)
  other arithmetic  2.33 us (6%)
    pallas_call x1, Pallas kernels, fused_body(): pl.pallas_call(fused_kernel, out_shape=jax.ShapeDtypeStruct(pair.shape, f...  33.7 us
    add x1, other arithmetic, fused_body(): return pair + change  2.33 us

profile of v4, /device:TPU:0, one launch (start us, length us, event | category | flops | bytes accessed | tf_op | source)
XLA Modules:
  0.0 36.1 jit_solution(18382882597566731260)
XLA Ops:
  0.0 0.0 copy-start
  0.0 33.7 %window.1 = f32[16,128,128]{2,1,0:T(8,128)} custom-call(f32[16,128,128]{2,1,0:T(8,128)} %pair_hbm.1, s32[1,128]{1,0:T(1,128)} %bitcast.10, bf16[256,128]{1,0:T(8,128)(2,1)} %bitcast.8, bf16[128,128]{1,0:T(8,128)(2,1)} %wog_hbm.1, bf16[128,128]{1,0:T(8,128)(2,1)} %wop_hbm.1, bf16[256,128]{1,0:T(8,128)(2,1)} %bitcast.9, bf16[2,128]{1,0:T(2,128)(2,1)} %bitcast.11, ...), custom_call_target="tpu_custom_call" | custom-call | tf_op jit(solution)/shard_map/window/pallas_call | solution.py:325
  33.7 0.0 copy-done
  33.8 2.3 %add.3 = f32[16,128,128]{2,1,0:T(8,128)} add(f32[16,128,128]{2,1,0:T(8,128)S(1)} %copy-done, f32[16,128,128]{2,1,0:T(8,128)} %window.1) | non-fusion elementwise | flops 262144 | bytes 3145728 | tf_op jit(solution)/shard_map/add | solution.py:384
Async XLA Ops:
  0.0 33.7 %copy-start = (f32[16,128,128]{2,1,0:T(8,128)S(1)}, f32[16,128,128]{2,1,0:T(8,128)}, u32[]{:S(2)}) copy-start(f32[16,128,128]{2,1,0:T(8,128)} %pair_hbm.1) | copy-start | bytes 3145732

commit v5 on v4

--- a/solution.py
+++ b/solution.py
@@ -184,6 +184,19 @@
                 l_copy(dg, c, place_to(dg), place_from(dg)).wait_recv()
             widen(wide_l, place_from(dg), got_l[place_from(dg)])
 
+    def b_copy(k, q, src, dst):
+        dg, d = around[k]
+        part = pl.ds(64 * q, 64)
+        return pltpu.make_async_remote_copy(
+            src_ref=back.at[src, part], dst_ref=owned.at[dst, part],
+            send_sem=b_send.at[k, q], recv_sem=b_recv.at[k, q],
+            device_id={"row": row_to(0, dg), "sub": peer_sub(d)}, device_id_type=MESH,
+        )
+
+    def b_part(k, q):
+        dg, d = around[k]
+        return b_copy(k, q, place_to(dg) * 2 + peer_sub(d), sub * 4 + place)
+
     for pair_of in range(8):
         sums = []
         for h in (2 * pair_of, 2 * pair_of + 1):
@@ -194,18 +207,13 @@
             )
             sums.append(total.reshape(8, 8, 128))
         back[:, pl.ds(16 * pair_of, 16), :] = jnp.concatenate(sums, axis=1).astype(jnp.bfloat16)
-
-    def b_copy(k, dg, d, src, dst):
-        return pltpu.make_async_remote_copy(
-            src_ref=back.at[src], dst_ref=owned.at[dst], send_sem=b_send.at[k], recv_sem=b_recv.at[k],
-            device_id={"row": row_to(0, dg), "sub": peer_sub(d)}, device_id_type=MESH,
-        )
+        if pair_of % 4 == 3:
+            for k in range(len(around)):
+                b_part(k, pair_of // 4).start()
 
     def widen2(at, block):
         wide2[pl.ds(pl.multiple_of(at * 128, 128), 128), :] = block.astype(jnp.float32)
 
-    for k, (dg, d) in enumerate(around):
-        b_copy(k, dg, d, place_to(dg) * 2 + peer_sub(d), sub * 4 + place).start()
     widen2(sub * 4 + place, back[place * 2 + sub])
 
     for k in range(3):
@@ -219,7 +227,8 @@
     for k in reversed(range(len(around))):
         dg, d = around[k]
         source = peer_sub(d) * 4 + place_from(dg)
-        b_copy(k, dg, d, 0, source).wait_recv()
+        for q in range(2):
+            b_copy(k, q, 0, source).wait_recv()
         widen2(source, owned[source])
 
     for i in range(half):
@@ -309,8 +318,9 @@
             r_copy(ds, dg, c, place_to(dg), row).wait_send()
             if ds == 0:
                 l_copy(dg, c, place_to(dg), place).wait_send()
-    for k, (dg, d) in enumerate(around):
-        b_copy(k, dg, d, place_to(dg) * 2 + peer_sub(d), sub * 4 + place).wait_send()
+    for k in range(len(around)):
+        for q in range(2):
+            b_part(k, q).wait_send()
     for k in range(len(every)):
         c_copy(k, mine).wait_send()
     for i in range(half):
@@ -368,7 +378,7 @@
             dma((3,)), dma((3,)),
             dma((4, CHUNKS)), dma((4, CHUNKS)),
             dma((8, CHUNKS)), dma((8, CHUNKS)),
-            dma((7,)), dma((7,)),
+            dma((7, 2)), dma((7, 2)),
             dma((15,)), dma((15,)),
             dma((8,)), dma((8,)), dma((8,)),
             pltpu.VMEM((8, 128, 128), f32),

time: 36.2 us -> 36.4 us (level)
  no operation moved by 1% of the time
where the time goes in v5:
time: 36.4 us; the launch traced here: 36.2 us
  Pallas kernels  33.9 us (93%)
  other arithmetic  2.33 us (6%)
    pallas_call x1, Pallas kernels, fused_body(): pl.pallas_call(fused_kernel, out_shape=jax.ShapeDtypeStruct(pair.shape, f...  33.9 us
    add x1, other arithmetic, fused_body(): return pair + change  2.33 us

profile of v5, /device:TPU:0, one launch (start us, length us, event | category | flops | bytes accessed | tf_op | source)
XLA Modules:
  0.0 36.2 jit_solution(407347808364308871)
XLA Ops:
  0.0 0.0 copy-start
  0.0 33.9 %window.1 = f32[16,128,128]{2,1,0:T(8,128)} custom-call(f32[16,128,128]{2,1,0:T(8,128)} %pair_hbm.1, s32[1,128]{1,0:T(1,128)} %bitcast.10, bf16[256,128]{1,0:T(8,128)(2,1)} %bitcast.8, bf16[128,128]{1,0:T(8,128)(2,1)} %wog_hbm.1, bf16[128,128]{1,0:T(8,128)(2,1)} %wop_hbm.1, bf16[256,128]{1,0:T(8,128)(2,1)} %bitcast.9, bf16[2,128]{1,0:T(2,128)(2,1)} %bitcast.11, ...), custom_call_target="tpu_custom_call" | custom-call | tf_op jit(solution)/shard_map/window/pallas_call | solution.py:335
  33.9 0.0 copy-done
  33.9 2.3 %add.3 = f32[16,128,128]{2,1,0:T(8,128)} add(f32[16,128,128]{2,1,0:T(8,128)S(1)} %copy-done, f32[16,128,128]{2,1,0:T(8,128)} %window.1) | non-fusion elementwise | flops 262144 | bytes 3145728 | tf_op jit(solution)/shard_map/add | solution.py:394
Async XLA Ops:
  0.0 33.9 %copy-start = (f32[16,128,128]{2,1,0:T(8,128)S(1)}, f32[16,128,128]{2,1,0:T(8,128)}, u32[]{:S(2)}) copy-start(f32[16,128,128]{2,1,0:T(8,128)} %pair_hbm.1) | copy-start | bytes 3145732
